TPU v7x, 32 devices: a whole 2x2x4 slice. The times are simulated.
32 devices in a mesh: groups: 2 (over y), batch: 4 (over z), pair: 2 (over x), sub: 2 (over core).
Axes of the slice: x: 2, y: 2, z: 4, core: 2. Of those that a mesh axis runs over, the one named last changes fastest.
Arguments:
- teacher_feats: bfloat16 [4096, 1024], P(('groups', 'batch', 'pair', 'sub')), parts along dimension 0, may hold values from -6 to 6
- student_feats: bfloat16 [4096, 384], P(('groups', 'batch', 'pair', 'sub')), parts along dimension 0, may hold values from -6 to 6
- head_weight: bfloat16 [384, 1024], replicated, may hold values from -0.3125 to 0.3125
- teacher_lse: float32 [4096], P(('groups', 'batch', 'pair', 'sub')), parts along dimension 0, may hold values from -1.5 to 1.5
- student_lse: float32 [4096], P(('groups', 'batch', 'pair', 'sub')), parts along dimension 0, may hold values from -1.5 to 1.5
Outputs:
- student_grad: bfloat16 [4096, 384], P(('groups', 'batch', 'pair', 'sub')), parts along dimension 0
- head_grad: float32 [768, 1024], P('groups'), parts along dimension 0
There are 2 independent parts, one for each index of `groups`. A program takes and returns all parts, laid end to end along the dimension named above; an argument that names none is the same for every part. Nothing has to cross between parts.
All inputs are finite; a program needn't handle non-finite values.
Results may differ from a plain program's by a relative error of at most 0.011.
Values may be sent and summed in bfloat16 or wider, within the bound.
A program may use at most 64 MiB of HBM per device.

v0:
```python
import jax
import jax.numpy as jnp
from jax import lax
from jax.sharding import PartitionSpec as P

TEACHER_TEMP = 0.04
STUDENT_TEMP = 0.05
LOSS_WEIGHT = 0.5
HEAD_SCALE = 0.0078125
EPSILON = 1e-06


def from_behind(value, axis, by):
    count = lax.axis_size(axis)
    return lax.ppermute(value, axis, [(i, (i + by) % count) for i in range(count)])


def from_partner(block, axis, distance):
    count = lax.axis_size(axis)
    route = []
    for low in range(count):
        high = low | 1 << distance
        if high != low and high < count:
            route += [(low, high), (high, low)]
    return lax.ppermute(block, axis, route)


def tile_grad(rows_t, rows_e, rows_s, cols_t, cols_e, cols_s):
    teacher_logits = (
        lax.dot_general(
            rows_t, cols_t, (((1,), (1,)), ((), ())), preferred_element_type=jnp.float32
        )
        / TEACHER_TEMP
    )
    student_logits = (
        lax.dot_general(
            rows_e, cols_e, (((1,), (1,)), ((), ())), preferred_element_type=jnp.float32
        )
        / STUDENT_TEMP
    )
    total = jnp.exp(student_logits - rows_s[:, 1:2]) - jnp.exp(teacher_logits - rows_s[:, 0:1])
    total = (
        total
        + jnp.exp(student_logits - cols_s[None, :, 1])
        - jnp.exp(teacher_logits - cols_s[None, :, 0])
    )
    return (total * (LOSS_WEIGHT / STUDENT_TEMP)).astype(jnp.bfloat16)


def body(teacher_feats, student_feats, head_weight, teacher_lse, student_lse):
    teacher_wide = teacher_feats.astype(jnp.float32)
    teacher_unit = (
        teacher_wide / jnp.sqrt(jnp.sum(teacher_wide * teacher_wide, 1, keepdims=True) + EPSILON)
    ).astype(jnp.bfloat16)
    projected = jnp.dot(student_feats, head_weight, preferred_element_type=jnp.float32)
    magnitude = jnp.sqrt(jnp.sum(projected * projected, 1, keepdims=True) + EPSILON)
    unit = projected / magnitude
    unit_bf = unit.astype(jnp.bfloat16)
    stats = jnp.stack([teacher_lse, student_lse], 1)
    panel_t, panel_e, panel_s = (
        lax.all_gather(teacher_unit, "pair", axis=0, tiled=True),
        lax.all_gather(unit_bf, "pair", axis=0, tiled=True),
        lax.all_gather(stats.astype(jnp.bfloat16), "pair", axis=0, tiled=True).astype(stats.dtype),
    )
    home_block = (
        lax.all_gather(teacher_unit, "sub", axis=0, tiled=True),
        lax.all_gather(unit_bf, "sub", axis=0, tiled=True),
        lax.all_gather(stats.astype(jnp.bfloat16), "sub", axis=0, tiled=True).astype(stats.dtype),
    )
    rounds = min(3, lax.axis_size("batch") - 1)
    row_totals = jnp.zeros((panel_e.shape[0], unit.shape[1]), jnp.float32)
    column_totals = jnp.zeros((home_block[1].shape[0], unit.shape[1]), jnp.float32)
    forward_piece = home_block
    for offset in range(1, rounds + 1):
        forward_piece = (
            from_behind(home_block[0], "batch", -offset),
            from_behind(home_block[1], "batch", -offset),
            from_behind(home_block[2].astype(jnp.bfloat16), "batch", -offset).astype(jnp.float32),
        )
        weights = tile_grad(
            panel_t, panel_e, panel_s, forward_piece[0], forward_piece[1], forward_piece[2]
        )
        row_totals = row_totals + jnp.dot(
            weights, forward_piece[1], preferred_element_type=jnp.float32
        )
        partner_terms = lax.dot_general(
            weights, panel_e, (((0,), (0,)), ((), ())), preferred_element_type=jnp.float32
        )
        column_totals = column_totals + from_behind(
            partner_terms.astype(jnp.bfloat16), "batch", offset
        ).astype(partner_terms.dtype)
    embed_grad = lax.psum_scatter(
        row_totals.astype(jnp.bfloat16), "pair", scatter_dimension=0, tiled=True
    ).astype(jnp.float32)
    own_rows = unit.shape[0]
    core = lax.axis_index("sub")
    mine = lax.dynamic_slice_in_dim(column_totals, core * own_rows, own_rows, 0)
    others = lax.dynamic_slice_in_dim(column_totals, (1 - core) * own_rows, own_rows, 0)
    embed_grad = embed_grad + (
        mine + from_partner(others.astype(jnp.bfloat16), "sub", 0).astype(others.dtype)
    )
    along = jnp.sum(unit * embed_grad, 1, keepdims=True)
    grad_proj = ((embed_grad - unit * along) / magnitude).astype(jnp.bfloat16)
    student_grad = lax.dot_general(
        grad_proj, head_weight, (((1,), (1,)), ((), ())), preferred_element_type=jnp.float32
    ).astype(jnp.bfloat16)
    local_head = lax.dot_general(
        student_feats, grad_proj, (((0,), (0,)), ((), ())), preferred_element_type=jnp.float32
    )
    head_grad = lax.psum(local_head, ("batch", "pair", "sub")) * HEAD_SCALE
    return (student_grad, head_grad)


def solution(mesh):
    in_specs = (
        P(("groups", "batch", "pair", "sub"), None),
        P(("groups", "batch", "pair", "sub"), None),
        P(),
        P(("groups", "batch", "pair", "sub")),
        P(("groups", "batch", "pair", "sub")),
    )
    out_specs = (P(("groups", "batch", "pair", "sub"), None), P("groups", None))
    return jax.shard_map(body, mesh=mesh, in_specs=in_specs, out_specs=out_specs, check_vma=False)
```

profile of v0, /device:TPU:9, one launch (start us, length us, event | category | flops | bytes accessed | tf_op | source)
XLA Modules:
  0.0 267.6 jit_solution(13775471749379499329)
XLA Ops:
  7.2 0.0 copy-start
  7.2 0.0 reduce-scatter.2.cloned.1.call-start
  7.2 1.1 copy-done
  8.3 1.3 multiply_reduce_fusion.1
  9.6 0.0 copy-start.4
  9.6 0.0 copy-start.5
  9.6 0.1 fusion.4
  9.7 2.5 all_gather.19
  12.2 1.3 collective-permute-start.6
  13.5 1.0 collective-permute-start.3
  14.5 0.1 fusion.2
  14.7 0.1 fusion.3
  14.8 2.5 all_gather.22
  17.3 0.6 collective-permute-start.7
  17.9 3.2 %collective-permute-start.4 = (bf16[256,1024]{1,0:T(8,128)(2,1)S(1)}, bf16[256,1024]{1,0:T(8,128)(2,1)S(1)}, u32[]{:S(2)}, u32[]{:S(2)}) collective-permute-start(bf16[256,1024]{1,0:T(8,128)(2,1)S(1)} %all_gather.22), channel_id=1, source_target_pairs={{0,8},{4,12},{8,0},{12,4},{1,9},{5,13},{9,1},{13,5},{2,10},{6,14},... | collective-permute-start | bytes 1572872 | tf_op jit(solution)/shard_map/ppermute | solution.py:15
  21.1 2.4 all_gather.23
  23.5 0.0 collective-permute-start.8
  23.5 8.3 %all_gather.18 = bf16[256,1024]{1,0:T(8,128)(2,1)S(1)} all-gather(bf16[128,1024]{1,0:T(8,128)(2,1)S(1)} %fusion.4), channel_id=1, replica_groups=mesh['groups'=2,'batch'=4,'pair'=2,'sub'=2] {'pair'}, dimensions={0}, use_global_device_ids=true | all-gather | bytes 786432 | tf_op jit(solution)/shard_map/all_gather | solution.py:62
  31.8 3.4 %all_gather.20 = bf16[256,2]{0,1:T(2,128)(2,1)S(1)} all-gather(bf16[128,2]{0,1:T(2,128)(2,1)S(1)} %pad_maximum_fusion), channel_id=1, replica_groups=mesh['groups'=2,'batch'=4,'pair'=2,'sub'=2] {'pair'}, dimensions={0}, use_global_device_ids=true | all-gather | bytes 1536 | tf_op jit(solution)/shard_map/all_gather | solution.py:63
  35.1 6.5 %all_gather.21 = bf16[256,1024]{1,0:T(8,128)(2,1)S(1)} all-gather(bf16[128,1024]{1,0:T(8,128)(2,1)S(1)} %fusion.3), channel_id=1, replica_groups=mesh['groups'=2,'batch'=4,'pair'=2,'sub'=2] {'pair'}, dimensions={0}, use_global_device_ids=true | all-gather | bytes 786432 | tf_op jit(solution)/shard_map/all_gather | solution.py:61
  41.6 39.1 %collective-permute-done.8 = bf16[256,2]{0,1:T(2,128)(2,1)S(1)} collective-permute-done((bf16[256,2]{0,1:T(2,128)(2,1)S(1)}, bf16[256,2]{0,1:T(2,128)(2,1)S(1)}, u32[]{:S(2)}, u32[]{:S(2)}) %collective-permute-start.8) | collective-permute-done | bytes 1056 | tf_op jit(solution)/shard_map/ppermute | solution.py:15
  80.7 0.0 collective-permute-start.5
  80.7 3.3 %collective-permute-done.5 = bf16[256,2]{0,1:T(2,128)(2,1)S(1)} collective-permute-done((bf16[256,2]{0,1:T(2,128)(2,1)S(1)}, bf16[256,2]{0,1:T(2,128)(2,1)S(1)}, u32[]{:S(2)}, u32[]{:S(2)}) %collective-permute-start.5) | collective-permute-done | bytes 1056 | tf_op jit(solution)/shard_map/ppermute | solution.py:15
  84.0 0.7 collective-permute-start.2
  84.7 2.1 collective-permute-done.2
  86.9 0.3 collective-permute-start
  87.2 0.0 collective-permute-done.6
  87.2 2.6 collective-permute-start.1
  89.8 0.3 convolution_multiply_fusion.1
  90.1 0.0 collective-permute-done.7
  90.1 0.4 multiply_convert_fusion
  90.6 1.1 convolution_convert_fusion
  91.7 0.9 collective-permute-start.11
  92.6 0.0 collective-permute-done.3
  92.6 0.3 convolution_multiply_fusion.3
  92.9 0.0 collective-permute-done.4
  93.0 0.4 multiply_convert_fusion.1
  93.4 1.1 convolution_convert_fusion.1
  94.5 0.0 collective-permute-start.10
  94.5 2.3 collective-permute-done
  96.8 0.3 convolution_multiply_fusion.5
  97.1 10.9 %collective-permute-done.1 = bf16[256,1024]{1,0:T(8,128)(2,1)S(1)} collective-permute-done((bf16[256,1024]{1,0:T(8,128)(2,1)S(1)}, bf16[256,1024]{1,0:T(8,128)(2,1)S(1)}, u32[]{:S(2)}, u32[]{:S(2)}) %collective-permute-start.1) | collective-permute-done | bytes 524320 | tf_op jit(solution)/shard_map/ppermute | solution.py:15
  108.0 0.4 multiply_convert_fusion.2
  108.4 0.3 convolution_convert_fusion.2
  108.8 1.2 collective-permute-start.9
  110.0 0.3 fusion.10
  110.3 0.3 fusion.9
  110.6 1.1 fusion.1
  111.7 0.0 reduce-scatter.2.cloned.1.call-update
  111.8 0.0 all-reduce.2.cloned.1.call-start
  111.8 7.4 %collective-permute-done.11 = bf16[256,1024]{1,0:T(8,128)(2,1)S(1)} collective-permute-done((bf16[256,1024]{1,0:T(8,128)(2,1)}, bf16[256,1024]{1,0:T(8,128)(2,1)S(1)}, u32[]{:S(2)}, u32[]{:S(2)}) %collective-permute-start.11) | collective-permute-done | bytes 524320 | tf_op jit(solution)/shard_map/ppermute | solution.py:15
  119.2 27.0 %collective-permute-done.10 = bf16[256,1024]{1,0:T(8,128)(2,1)S(1)} collective-permute-done((bf16[256,1024]{1,0:T(8,128)(2,1)}, bf16[256,1024]{1,0:T(8,128)(2,1)S(1)}, u32[]{:S(2)}, u32[]{:S(2)}) %collective-permute-start.10) | collective-permute-done | bytes 524320 | tf_op jit(solution)/shard_map/ppermute | solution.py:15
  146.2 11.1 %collective-permute-done.9 = bf16[256,1024]{1,0:T(8,128)(2,1)} collective-permute-done((bf16[256,1024]{1,0:T(8,128)(2,1)S(1)}, bf16[256,1024]{1,0:T(8,128)(2,1)}, u32[]{:S(2)}, u32[]{:S(2)}) %collective-permute-start.9) | collective-permute-done | bytes 524320 | tf_op jit(solution)/shard_map/ppermute | solution.py:15
  157.4 1.3 convert_add_fusion
  158.7 0.6 collective-permute-start.12
  159.3 1.2 collective-permute-done.12
  160.4 1.2 multiply_reduce_fusion
  161.7 0.2 divide_convert_fusion
  161.9 1.5 convolution_bitcast_fusion
  163.4 0.0 all-reduce.2.cloned.1.call-update
  163.4 1.0 convolution_convert_fusion.3
  164.4 93.2 %all-reduce.2.cloned.1.call-done = f32[384,1024]{0,1:T(8,128)} async-done(((f32[384,1024]{0,1:T(8,128)}), f32[384,1024]{0,1:T(8,128)}) %all-reduce.2.cloned.1.call-update) | async-done | bytes 1572880 | tf_op jit(solution)/shard_map/psum | solution.py:110
  257.7 1.5 broadcast_multiply_fusion
  259.2 1.6 copy.7
  (18 shorter events, 0.1 us)
Async XLA Ops:
  7.2 1.1 copy-start
  7.2 7.3 %copy-start.1 = (bf16[128,1024]{1,0:T(8,128)(2,1)S(1)}, bf16[128,1024]{1,0:T(8,128)(2,1)}, u32[]{:S(2)}) copy-start(bf16[128,1024]{1,0:T(8,128)(2,1)} %param.5) | copy-start | bytes 786436
  7.2 153.2 %reduce-scatter.2.cloned.1.call-start = ((), (), s32[]{:S(2)}) async-start(), calls=%async_computation.1 | async-start | bytes 786432 | tf_op jit(solution)/shard_map/reduce_scatter | solution.py:92
  9.6 11.5 %copy-start.4 = (f32[128]{0:T(128)S(1)}, f32[128]{0:T(128)}, u32[]{:S(2)}) copy-start(f32[128]{0:T(128)} %param.9) | copy-start | bytes 1540
  9.6 11.5 %copy-start.5 = (f32[128]{0:T(128)S(1)}, f32[128]{0:T(128)}, u32[]{:S(2)}) copy-start(f32[128]{0:T(128)} %param.8) | copy-start | bytes 1540
  12.2 74.9 %collective-permute-start.6 = (bf16[256,1024]{1,0:T(8,128)(2,1)S(1)}, bf16[256,1024]{1,0:T(8,128)(2,1)S(1)}, u32[]{:S(2)}, u32[]{:S(2)}) collective-permute-start(bf16[256,1024]{1,0:T(8,128)(2,1)S(1)} %all_gather.19), channel_id=1, source_target_pairs={{0,4},{4,8},{8,12},{12,0},{1,5},{5,9},{9,13},{13,1},{2,6},{6,10},{... | collective-permute-start | bytes 1572872 | tf_op jit(solution)/shard_map/ppermute | solution.py:15
  13.5 79.1 %collective-permute-start.3 = (bf16[256,1024]{1,0:T(8,128)(2,1)S(1)}, bf16[256,1024]{1,0:T(8,128)(2,1)S(1)}, u32[]{:S(2)}, u32[]{:S(2)}) collective-permute-start(bf16[256,1024]{1,0:T(8,128)(2,1)S(1)} %all_gather.19), channel_id=1, source_target_pairs={{0,8},{4,12},{8,0},{12,4},{1,9},{5,13},{9,1},{13,5},{2,10},{6,14},... | collective-permute-start | bytes 1572872 | tf_op jit(solution)/shard_map/ppermute | solution.py:15
  17.3 72.9 %collective-permute-start.7 = (bf16[256,1024]{1,0:T(8,128)(2,1)S(1)}, bf16[256,1024]{1,0:T(8,128)(2,1)S(1)}, u32[]{:S(2)}, u32[]{:S(2)}) collective-permute-start(bf16[256,1024]{1,0:T(8,128)(2,1)S(1)} %all_gather.22), channel_id=1, source_target_pairs={{0,4},{4,8},{8,12},{12,0},{1,5},{5,9},{9,13},{13,1},{2,6},{6,10},{... | collective-permute-start | bytes 1572872 | tf_op jit(solution)/shard_map/ppermute | solution.py:15
  17.9 75.1 %collective-permute-start.4 = (bf16[256,1024]{1,0:T(8,128)(2,1)S(1)}, bf16[256,1024]{1,0:T(8,128)(2,1)S(1)}, u32[]{:S(2)}, u32[]{:S(2)}) collective-permute-start(bf16[256,1024]{1,0:T(8,128)(2,1)S(1)} %all_gather.22), channel_id=1, source_target_pairs={{0,8},{4,12},{8,0},{12,4},{1,9},{5,13},{9,1},{13,5},{2,10},{6,14},... | collective-permute-start | bytes 1572872 | tf_op jit(solution)/shard_map/ppermute | solution.py:15
  23.5 57.2 %collective-permute-start.8 = (bf16[256,2]{0,1:T(2,128)(2,1)S(1)}, bf16[256,2]{0,1:T(2,128)(2,1)S(1)}, u32[]{:S(2)}, u32[]{:S(2)}) collective-permute-start(bf16[256,2]{0,1:T(2,128)(2,1)S(1)} %all_gather.23), channel_id=1, source_target_pairs={{0,4},{4,8},{8,12},{12,0},{1,5},{5,9},{9,13},{13,1},{2,6},{6,10},{... | collective-permute-start | bytes 3080 | tf_op jit(solution)/shard_map/ppermute | solution.py:15
  80.7 3.3 %collective-permute-start.5 = (bf16[256,2]{0,1:T(2,128)(2,1)S(1)}, bf16[256,2]{0,1:T(2,128)(2,1)S(1)}, u32[]{:S(2)}, u32[]{:S(2)}) collective-permute-start(bf16[256,2]{0,1:T(2,128)(2,1)S(1)} %all_gather.23), channel_id=1, source_target_pairs={{0,8},{4,12},{8,0},{12,4},{1,9},{5,13},{9,1},{13,5},{2,10},{6,14},... | collective-permute-start | bytes 3080 | tf_op jit(solution)/shard_map/ppermute | solution.py:15
  84.0 2.9 %collective-permute-start.2 = (bf16[256,2]{0,1:T(2,128)(2,1)S(1)}, bf16[256,2]{0,1:T(2,128)(2,1)S(1)}, u32[]{:S(2)}, u32[]{:S(2)}) collective-permute-start(bf16[256,2]{0,1:T(2,128)(2,1)S(1)} %all_gather.23), channel_id=1, source_target_pairs={{0,12},{4,0},{8,4},{12,8},{1,13},{5,1},{9,5},{13,9},{2,14},{6,2},{... | collective-permute-start | bytes 3080 | tf_op jit(solution)/shard_map/ppermute | solution.py:15
  86.9 9.9 %collective-permute-start = (bf16[256,1024]{1,0:T(8,128)(2,1)S(1)}, bf16[256,1024]{1,0:T(8,128)(2,1)S(1)}, u32[]{:S(2)}, u32[]{:S(2)}) collective-permute-start(bf16[256,1024]{1,0:T(8,128)(2,1)S(1)} %all_gather.19), channel_id=1, source_target_pairs={{0,12},{4,0},{8,4},{12,8},{1,13},{5,1},{9,5},{13,9},{2,14},{6,2},{... | collective-permute-start | bytes 1572872 | tf_op jit(solution)/shard_map/ppermute | solution.py:15
  87.2 20.9 %collective-permute-start.1 = (bf16[256,1024]{1,0:T(8,128)(2,1)S(1)}, bf16[256,1024]{1,0:T(8,128)(2,1)S(1)}, u32[]{:S(2)}, u32[]{:S(2)}) collective-permute-start(bf16[256,1024]{1,0:T(8,128)(2,1)S(1)} %all_gather.22), channel_id=1, source_target_pairs={{0,12},{4,0},{8,4},{12,8},{1,13},{5,1},{9,5},{13,9},{2,14},{6,2},{... | collective-permute-start | bytes 1572872 | tf_op jit(solution)/shard_map/ppermute | solution.py:15
  91.7 27.6 %collective-permute-start.11 = (bf16[256,1024]{1,0:T(8,128)(2,1)}, bf16[256,1024]{1,0:T(8,128)(2,1)S(1)}, u32[]{:S(2)}, u32[]{:S(2)}) collective-permute-start(bf16[256,1024]{1,0:T(8,128)(2,1)} %convolution_convert_fusion), channel_id=1, source_target_pairs={{0,12},{4,0},{8,4},{12,8},{1,13},{5,1},{9,5},{13,9},{2,14},{6,2},{... | collective-permute-start | bytes 1572872 | tf_op jit(solution)/shard_map/ppermute | solution.py:15
  94.5 51.7 %collective-permute-start.10 = (bf16[256,1024]{1,0:T(8,128)(2,1)}, bf16[256,1024]{1,0:T(8,128)(2,1)S(1)}, u32[]{:S(2)}, u32[]{:S(2)}) collective-permute-start(bf16[256,1024]{1,0:T(8,128)(2,1)} %convolution_convert_fusion.1), channel_id=1, source_target_pairs={{0,8},{4,12},{8,0},{12,4},{1,9},{5,13},{9,1},{13,5},{2,10},{6,14},... | collective-permute-start | bytes 1572872 | tf_op jit(solution)/shard_map/ppermute | solution.py:15
  108.8 48.6 %collective-permute-start.9 = (bf16[256,1024]{1,0:T(8,128)(2,1)S(1)}, bf16[256,1024]{1,0:T(8,128)(2,1)}, u32[]{:S(2)}, u32[]{:S(2)}) collective-permute-start(bf16[256,1024]{1,0:T(8,128)(2,1)S(1)} %convolution_convert_fusion.2), channel_id=1, source_target_pairs={{0,4},{4,8},{8,12},{12,0},{1,5},{5,9},{9,13},{13,1},{2,6},{6,10},{... | collective-permute-start | bytes 1572872 | tf_op jit(solution)/shard_map/ppermute | solution.py:15
  111.8 145.9 %all-reduce.2.cloned.1.call-start = ((), (), s32[]{:S(2)}) async-start(), calls=%async_computation.2 | async-start | bytes 3145728 | tf_op jit(solution)/shard_map/psum | solution.py:110
  158.7 1.7 collective-permute-start.12
  159.3 2.6 copy-start.3
  160.4 1.2 copy-start.2
Sparse Core Ops, SparseCore 0:
  111.9 23.6 reduce-scatter.1
  163.5 94.0 all-reduce.1
where the time goes:
time: 272 us; the launch traced here: 268 us
  waiting for transfers between devices  198 us (73%)
  blocking collectives  25.4 us (9%)
  between operations  14.2 us (5%)
  starting transfers between devices  12.6 us (5%)
  matrix products  10.4 us (4%)
  other arithmetic  4.6 us (2%)
  local copies, waits for them, and re-layouts  2.77 us (1%)
    ppermute x12, waiting for transfers between devices, from_behind(): lax.ppermute(value, axis, [(i, (i + by) % count) for i in range(count)])  103 us
    psum x1, waiting for transfers between devices, body(): head_grad = lax.psum(local_head, ('batch', 'pair', 'sub')) * HEAD_SCALE  93.2 us
    ppermute x12, starting transfers between devices, from_behind(): lax.ppermute(value, axis, [(i, (i + by) % count) for i in range(count)])  11.9 us
    all_gather x1, blocking collectives, body(): lax.all_gather(unit_bf, 'pair', axis=0, tiled=True)  8.26 us
    all_gather x1, blocking collectives, body(): lax.all_gather(teacher_unit, 'pair', axis=0, tiled=True)  6.48 us
  transfers between devices with their start and end apart: 15, of which 10 were waited for; matrix products, arithmetic and copies ran while one was open for 3% of the time, Pallas kernels for 0%

commit v1 on v0

v1 whole, which is shorter than its diff:
```python
import functools

import jax
import jax.numpy as jnp
from jax import lax
from jax.experimental import pallas as pl
from jax.experimental.pallas import tpu as pltpu
from jax.sharding import PartitionSpec as P

TEACHER_TEMP = 0.04
STUDENT_TEMP = 0.05
LOSS_WEIGHT = 0.5
HEAD_SCALE = 0.0078125
EPSILON = 1e-06
ROUNDS = 3
LANES = 128
CHUNKS = 2
STAT_ROWS = 16
MESH = pl.DeviceIdType.MESH
BF = jnp.bfloat16
F32 = jnp.float32


def nt(a, b):
    return lax.dot_general(a, b, (((1,), (1,)), ((), ())), preferred_element_type=F32)


def tn(a, b):
    return lax.dot_general(a, b, (((0,), (0,)), ((), ())), preferred_element_type=F32)


def project(feats, head):
    projected = jnp.dot(feats, head, preferred_element_type=F32)
    magnitude = jnp.sqrt(jnp.sum(projected * projected, 1, keepdims=True) + EPSILON)
    return projected / magnitude, magnitude


def kernel(
    n_batch, n_pair, tf_ref, sf_ref, hw_ref, tl_ref, sl_ref, sg_ref, head_ref,
    own, buf, t_own, u_own, unit_ref, acc, z_send, x_send, s_send, recv,
):
    rows, wide = tf_ref.shape
    sdim = sf_ref.shape[1]
    per = rows // CHUNKS
    t_tiles, s_tiles = wide // LANES, sdim // LANES
    stat_at = (t_tiles + s_tiles) * per
    hops = min(ROUNDS, n_batch - 1)
    ring = n_batch > 2 * ROUNDS
    times = 1.0 if ring else 2.0
    b, p, s = lax.axis_index("batch"), lax.axis_index("pair"), lax.axis_index("sub")

    def place(index):
        return lax.rem(index + n_batch, n_batch) if ring else index

    def when(index):
        if ring:
            return lambda f: f()
        return pl.when(jnp.logical_and(index >= 0, index < n_batch))

    barrier = pltpu.get_barrier_semaphore()
    for sign in (1, -1):
        @when(b + sign)
        def _():
            pl.semaphore_signal(
                barrier, inc=1, device_id={"batch": place(b + sign)}, device_id_type=MESH
            )
    for k in range(1, n_pair):
        pl.semaphore_signal(
            barrier, inc=1, device_id={"pair": lax.rem(p + k, n_pair)}, device_id_type=MESH
        )
    pl.semaphore_signal(barrier, inc=1, device_id={"sub": 1 - s}, device_id_type=MESH)

    wide_t = tf_ref[...].astype(F32)
    teacher = (
        wide_t / jnp.sqrt(jnp.sum(wide_t * wide_t, 1, keepdims=True) + EPSILON)
    ).astype(BF)
    t_own[...] = teacher
    stat_t, stat_s = jnp.exp(-tl_ref[...]), jnp.exp(-sl_ref[...])
    stat = jnp.concatenate([stat_t, stat_s, jnp.zeros((6, LANES), F32)], 0)
    high = stat.astype(BF)
    low = (stat - high.astype(F32)).astype(BF)
    stats = jnp.concatenate([high, low], 0)
    for q in range(CHUNKS):
        for k in range(t_tiles):
            own[q, k * per : (k + 1) * per, :] = teacher[
                q * per : (q + 1) * per, k * LANES : (k + 1) * LANES
            ]
        for k in range(s_tiles):
            at = (t_tiles + k) * per
            own[q, at : at + per, :] = sf_ref[
                q * per : (q + 1) * per, k * LANES : (k + 1) * LANES
            ]
        own[q, stat_at : stat_at + STAT_ROWS, :] = stats

    peers = n_pair + 2
    if not ring:
        peers = n_pair + jnp.minimum(b, 1) + jnp.minimum(n_batch - 1 - b, 1)
    pl.semaphore_wait(barrier, peers)

    def z_copy(d, h, q, src):
        return pltpu.make_async_remote_copy(
            src_ref=src,
            dst_ref=buf.at[d, h, p, s, q],
            send_sem=z_send.at[d, h, q],
            recv_sem=recv.at[d, h, p, s, q],
            device_id={"batch": place(b + 1 - 2 * d)},
            device_id_type=MESH,
        )

    def x_copy(d, h, q, k):
        return pltpu.make_async_remote_copy(
            src_ref=buf.at[d, h, p, s, q],
            dst_ref=buf.at[d, h, p, s, q],
            send_sem=x_send.at[d, h, k, q],
            recv_sem=recv.at[d, h, p, s, q],
            device_id={"pair": lax.rem(p + k, n_pair)},
            device_id_type=MESH,
        )

    def s_copy(d, h, q, source):
        return pltpu.make_async_remote_copy(
            src_ref=buf.at[d, h, source, s, q],
            dst_ref=buf.at[d, h, source, s, q],
            send_sem=s_send.at[d, h, source, q],
            recv_sem=recv.at[d, h, source, s, q],
            device_id={"sub": 1 - s},
            device_id_type=MESH,
        )

    def arrived(d, h, source, core, q):
        pltpu.make_async_remote_copy(
            src_ref=buf.at[d, h, source, core, q],
            dst_ref=buf.at[d, h, source, core, q],
            send_sem=s_send.at[d, h, source, q],
            recv_sem=recv.at[d, h, source, core, q],
            device_id={"sub": 1 - s},
            device_id_type=MESH,
        ).wait_recv()

    for q in range(CHUNKS):
        for d in range(2):
            @when(b + 1 - 2 * d)
            def _():
                z_copy(d, 0, q, own.at[q]).start()

    unit, magnitude = project(sf_ref[...], hw_ref[...])
    unit_ref[...] = unit
    u_own[...] = unit.astype(BF)
    acc[...] = jnp.zeros_like(acc)
    tall = stat.T
    row_t, row_s = tall[:, 0:1], tall[:, 1:2]

    def source_of(d, h):
        return b - (1 - 2 * d) * (h + 1)

    def z_step(h, q):
        def each(d, carry):
            @when(source_of(d, h))
            def _():
                arrived(d, h, p, s, q)

                @pl.when(h < hops - 1)
                def _():
                    @when(b + 1 - 2 * d)
                    def _():
                        z_copy(d, h + 1, q, buf.at[d, h, p, s, q]).start()

                for k in range(1, n_pair):
                    x_copy(d, h, q, k).start()
                s_copy(d, h, q, p).start()
            return carry

        lax.fori_loop(0, 2, each, 0)

    def x_step(h, q):
        def each(d, carry):
            @when(source_of(d, h))
            def _():
                for k in range(1, n_pair):
                    source = lax.rem(p + k, n_pair)
                    arrived(d, h, source, s, q)
                    s_copy(d, h, q, source).start()
            return carry

        lax.fori_loop(0, 2, each, 0)

    def tile(d, h, source):
        for q in range(CHUNKS):
            arrived(d, h, source, 1 - s, q)
        t_parts, f_parts, st = [], [], []
        for core in range(2):
            for q in range(CHUNKS):
                t_parts.append(jnp.concatenate(
                    [buf[d, h, source, core, q, k * per : (k + 1) * per, :] for k in range(t_tiles)], 1
                ))
                f_parts.append(jnp.concatenate(
                    [
                        buf[d, h, source, core, q, (t_tiles + k) * per : (t_tiles + k + 1) * per, :]
                        for k in range(s_tiles)
                    ], 1
                ))
            raw = buf[d, h, source, core, 0, stat_at : stat_at + STAT_ROWS, :].astype(F32)
            st.append(raw[0:8] + raw[8:16])
        cols_t = jnp.concatenate(t_parts, 0)
        cols_f = jnp.concatenate(f_parts, 0)
        cols_s = jnp.concatenate(st, 1)
        cols_u = project(cols_f, hw_ref[...])[0].astype(BF)
        zt = nt(t_own[...], cols_t) * (1.0 / TEACHER_TEMP)
        zs = nt(u_own[...], cols_u) * (1.0 / STUDENT_TEMP)
        g = jnp.exp(zs) * (row_s + cols_s[1:2]) - jnp.exp(zt) * (row_t + cols_s[0:1])
        weights = (g * (LOSS_WEIGHT / STUDENT_TEMP)).astype(BF)
        acc[...] += jnp.dot(weights, cols_u, preferred_element_type=F32)

    def work(h, first, last):
        def each(d, carry):
            @when(source_of(d, h))
            def _():
                def one(k, c):
                    tile(d, h, lax.rem(p + k, n_pair))
                    return c

                lax.fori_loop(first, last, one, 0)
            return carry

        lax.fori_loop(0, 2, each, 0)

    def stage(h, carry):
        for q in range(CHUNKS):
            @pl.when(h < hops)
            def _():
                z_step(h, q)

            if q == 0:
                @pl.when(h > 0)
                def _():
                    x_step(h - 1, CHUNKS - 1)
                    work(h - 1, 0, n_pair)
            else:
                @pl.when(h < hops)
                def _():
                    x_step(h, q - 1)
        return carry

    lax.fori_loop(0, hops + 1, stage, 0)

    embed = acc[...] * times
    unit = unit_ref[...]
    along = jnp.sum(unit * embed, 1, keepdims=True)
    grad_proj = ((embed - unit * along) / magnitude).astype(BF)
    sg_ref[...] = nt(grad_proj, hw_ref[...]).astype(BF)
    head_ref[...] = tn(sf_ref[...], grad_proj)

    for d in range(2):
        @when(b + 1 - 2 * d)
        def _():
            for q in range(CHUNKS):
                z_copy(d, 0, q, own.at[q]).wait_send()
        for h in range(hops):
            @when(source_of(d, h))
            def _():
                for q in range(CHUNKS):
                    if h < hops - 1:
                        @when(b + 1 - 2 * d)
                        def _():
                            z_copy(d, h + 1, q, buf.at[d, h, p, s, q]).wait_send()
                    for k in range(1, n_pair):
                        x_copy(d, h, q, k).wait_send()
                    for k in range(n_pair):
                        s_copy(d, h, q, lax.rem(p + k, n_pair)).wait_send()


def solution(mesh):
    n_batch, n_pair = mesh.shape["batch"], mesh.shape["pair"]
    hops = min(ROUNDS, n_batch - 1)

    def body(teacher_feats, student_feats, head_weight, teacher_lse, student_lse):
        rows, wide = teacher_feats.shape
        sdim, edim = head_weight.shape
        depth = (wide + sdim) // LANES * (rows // CHUNKS) + STAT_ROWS
        vmem = pl.BlockSpec(memory_space=pltpu.VMEM)
        student_grad, local_head = pl.pallas_call(
            functools.partial(kernel, n_batch, n_pair),
            out_shape=(
                jax.ShapeDtypeStruct((rows, sdim), BF),
                jax.ShapeDtypeStruct((sdim, edim), F32),
            ),
            in_specs=[vmem] * 5,
            out_specs=(vmem, vmem),
            scratch_shapes=[
                pltpu.VMEM((CHUNKS, depth, LANES), BF),
                pltpu.VMEM((2, hops, n_pair, 2, CHUNKS, depth, LANES), BF),
                pltpu.VMEM((rows, wide), BF),
                pltpu.VMEM((rows, edim), BF),
                pltpu.VMEM((rows, edim), F32),
                pltpu.VMEM((rows, edim), F32),
                pltpu.SemaphoreType.DMA((2, hops, CHUNKS)),
                pltpu.SemaphoreType.DMA((2, hops, n_pair, CHUNKS)),
                pltpu.SemaphoreType.DMA((2, hops, n_pair, CHUNKS)),
                pltpu.SemaphoreType.DMA((2, hops, n_pair, 2, CHUNKS)),
            ],
            compiler_params=pltpu.CompilerParams(
                collective_id=0, has_side_effects=True, vmem_limit_bytes=56 * 1024 * 1024
            ),
        )(
            teacher_feats, student_feats, head_weight,
            teacher_lse.reshape(1, rows), student_lse.reshape(1, rows),
        )
        head_grad = lax.psum(local_head, ("batch", "pair", "sub")) * HEAD_SCALE
        return student_grad, head_grad

    in_specs = (
        P(("groups", "batch", "pair", "sub"), None),
        P(("groups", "batch", "pair", "sub"), None),
        P(),
        P(("groups", "batch", "pair", "sub")),
        P(("groups", "batch", "pair", "sub")),
    )
    out_specs = (P(("groups", "batch", "pair", "sub"), None), P("groups", None))
    return jax.shard_map(body, mesh=mesh, in_specs=in_specs, out_specs=out_specs, check_vma=False)
```

time: 272 us -> 160 us (0.59)
  the two profiles are of different devices: /device:TPU:9 before, /device:TPU:0 now
where the time goes in v1:
time: 160 us
  waiting for transfers between devices  95.6 us (60%)
  Pallas kernels  47.1 us (29%)
  between operations  14 us (9%)
  other arithmetic  2.75 us (2%)
    psum x1, waiting for transfers between devices, body(): head_grad = lax.psum(local_head, ('batch', 'pair', 'sub')) * HEAD_SCALE  95.6 us
    pallas_call x1, Pallas kernels, body(): pl.pallas_call(functools.partial(kernel, n_batch, n_pair), out_shape=(jax...  47.1 us
  transfers between devices with their start and end apart: 1, of which 1 were waited for; matrix products, arithmetic and copies ran while one was open for 0% of the time, Pallas kernels for 0%

profile of v1, /device:TPU:0, one launch (start us, length us, event | category | flops | bytes accessed | tf_op | source)
XLA Modules:
  0.0 160.2 jit_solution(11968212671275021117)
XLA Ops:
  7.2 0.0 all-reduce.2.cloned.1.call-start
  7.2 47.1 %shard_map.68 = (bf16[128,384]{1,0:T(8,128)(2,1)}, f32[384,1024]{1,0:T(8,128)}) custom-call(bf16[128,1024]{1,0:T(8,128)(2,1)} %tf_ref.1, bf16[128,384]{1,0:T(8,128)(2,1)} %sf_ref.1, bf16[384,1024]{1,0:T(8,128)(2,1)} %hw_ref.1, f32[1,128]{1,0:T(1,128)} %bitcast.2, f32[1,128]{1,0:T(1,128)} %bitcast.3), custom_call_target="tpu_custom_call" | custom-call | tf_op jit(solution)/shard_map/pallas_call | solution.py:281
  54.3 0.0 all-reduce.2.cloned.1.call-update
  54.4 0.0 copy-start
  54.4 95.6 %all-reduce.2.cloned.1.call-done = f32[384,1024]{1,0:T(8,128)} async-done(((f32[384,1024]{1,0:T(8,128)}), f32[384,1024]{1,0:T(8,128)}) %all-reduce.2.cloned.1.call-update) | async-done | bytes 1572880 | tf_op jit(solution)/shard_map/psum | solution.py:308
  150.0 2.8 %broadcast_multiply_fusion = f32[384,1024]{1,0:T(8,128)} fusion(f32[384,1024]{1,0:T(8,128)} %all-reduce.2.cloned.1.call-done), kind=kLoop, calls=%fused_computation | loop fusion | flops 393216 | bytes 3145728 | tf_op jit(solution)/shard_map/mul | solution.py:308
  152.8 0.0 copy-done
  152.8 0.6 copy.9
Async XLA Ops:
  7.2 142.8 %all-reduce.2.cloned.1.call-start = ((), (), s32[]{:S(2)}) async-start(), calls=%async_computation | async-start | bytes 3145728 | tf_op jit(solution)/shard_map/psum | solution.py:308
  54.4 98.4 %copy-start = (bf16[128,384]{1,0:T(8,128)(2,1)S(1)}, bf16[128,384]{1,0:T(8,128)(2,1)}, u32[]{:S(2)}) copy-start(bf16[128,384]{1,0:T(8,128)(2,1)} %get-tuple-element.8) | copy-start | bytes 294916
Sparse Core Ops, SparseCore 0:
  54.5 95.4 all-reduce.1

commit v2 on v1

--- a/solution.py
+++ b/solution.py
@@ -37,7 +37,9 @@
 
 def kernel(
     n_batch, n_pair, tf_ref, sf_ref, hw_ref, tl_ref, sl_ref, sg_ref, head_ref,
-    own, buf, t_own, u_own, unit_ref, acc, z_send, x_send, s_send, recv,
+    own, buf, t_own, u_own, unit_ref, acc, part, half_out, half_in, mine, chunks, sums,
+    z_send, x_send, s_send, recv,
+    half_send, half_recv, c_send, c_recv, b_send, b_recv, f_send,
 ):
     rows, wide = tf_ref.shape
     sdim = sf_ref.shape[1]
@@ -57,17 +59,31 @@
             return lambda f: f()
         return pl.when(jnp.logical_and(index >= 0, index < n_batch))
 
+    chips = n_batch * n_pair
+    chip = b * n_pair + p
+    tiles, half, _ = half_out.shape
+    piece = chunks.shape[1]
+    owners = sums.shape[1]
+
+    def at_chip(index):
+        return {"batch": index // n_pair, "pair": lax.rem(index, n_pair)}
+
+    def owns(index):
+        return pl.when(index < owners) if owners < chips else lambda f: f()
+
+    def others(f):
+        def one(k, carry):
+            f(lax.rem(chip + k, chips))
+            return carry
+
+        lax.fori_loop(1, chips, one, 0)
+
     barrier = pltpu.get_barrier_semaphore()
-    for sign in (1, -1):
-        @when(b + sign)
-        def _():
-            pl.semaphore_signal(
-                barrier, inc=1, device_id={"batch": place(b + sign)}, device_id_type=MESH
-            )
-    for k in range(1, n_pair):
-        pl.semaphore_signal(
-            barrier, inc=1, device_id={"pair": lax.rem(p + k, n_pair)}, device_id_type=MESH
-        )
+
+    def greet(other):
+        pl.semaphore_signal(barrier, inc=1, device_id=at_chip(other), device_id_type=MESH)
+
+    others(greet)
     pl.semaphore_signal(barrier, inc=1, device_id={"sub": 1 - s}, device_id_type=MESH)
 
     wide_t = tf_ref[...].astype(F32)
@@ -92,10 +108,7 @@
             ]
         own[q, stat_at : stat_at + STAT_ROWS, :] = stats
 
-    peers = n_pair + 2
-    if not ring:
-        peers = n_pair + jnp.minimum(b, 1) + jnp.minimum(n_batch - 1 - b, 1)
-    pl.semaphore_wait(barrier, peers)
+    pl.semaphore_wait(barrier, chips)
 
     def z_copy(d, h, q, src):
         return pltpu.make_async_remote_copy(
@@ -247,8 +260,103 @@
     unit = unit_ref[...]
     along = jnp.sum(unit * embed, 1, keepdims=True)
     grad_proj = ((embed - unit * along) / magnitude).astype(BF)
+    local = tn(sf_ref[...], grad_proj)
+    for k in range(tiles):
+        part[k] = local[:, k * LANES : (k + 1) * LANES]
+
+    here = pl.ds(pl.multiple_of(s * half, STAT_ROWS), half)
+    there = pl.ds(pl.multiple_of((1 - s) * half, STAT_ROWS), half)
+    half_out[...] = part[:, there, :].astype(BF)
+    swap = pltpu.make_async_remote_copy(
+        src_ref=half_out, dst_ref=half_in, send_sem=half_send.at[0], recv_sem=half_recv.at[0],
+        device_id={"sub": 1 - s}, device_id_type=MESH,
+    )
+    swap.start()
     sg_ref[...] = nt(grad_proj, hw_ref[...]).astype(BF)
-    head_ref[...] = tn(sf_ref[...], grad_proj)
+    swap.wait()
+    part[:, here, :] = part[:, here, :] + half_in[...].astype(F32)
+    mine[...] = part[:, here, :].astype(BF)
+
+    def piece_of(index):
+        return lax.rem(index, tiles), index // tiles * piece
+
+    def c_copy(owner, source):
+        tile_at, row_at = piece_of(owner)
+        return pltpu.make_async_remote_copy(
+            src_ref=mine.at[tile_at, pl.ds(pl.multiple_of(row_at, STAT_ROWS), piece)],
+            dst_ref=chunks.at[source],
+            send_sem=c_send.at[owner], recv_sem=c_recv.at[source],
+            device_id=at_chip(owner), device_id_type=MESH,
+        )
+
+    def b_copy(other, source):
+        return pltpu.make_async_remote_copy(
+            src_ref=sums.at[s, source], dst_ref=sums.at[s, source],
+            send_sem=b_send.at[other], recv_sem=b_recv.at[s, source],
+            device_id=at_chip(other), device_id_type=MESH,
+        )
+
+    def f_copy(source, core):
+        return pltpu.make_async_remote_copy(
+            src_ref=sums.at[core, source], dst_ref=sums.at[core, source],
+            send_sem=f_send.at[source], recv_sem=b_recv.at[core, source],
+            device_id={"sub": 1 - s}, device_id_type=MESH,
+        )
+
+    def scatter(owner):
+        @owns(owner)
+        def _():
+            c_copy(owner, chip).start()
+
+    others(scatter)
+
+    @owns(chip)
+    def _():
+        tile_at, row_at = piece_of(chip)
+        first = part[tile_at, pl.ds(pl.multiple_of(s * half + row_at, STAT_ROWS), piece), :]
+
+        def add(k, total):
+            source = lax.rem(chip + k, chips)
+            c_copy(chip, source).wait_recv()
+            return total + chunks[source].astype(F32)
+
+        sums[s, chip] = lax.fori_loop(1, chips, add, first).astype(BF)
+        others(lambda other: b_copy(other, chip).start())
+        f_copy(chip, s).start()
+
+    def pass_on(source):
+        @owns(source)
+        def _():
+            b_copy(source, source).wait_recv()
+            f_copy(source, s).start()
+
+    others(pass_on)
+
+    def place_piece(core, source):
+        tile_at, row_at = source % tiles, source // tiles * piece
+        head_ref[
+            core * half + row_at : core * half + row_at + piece,
+            tile_at * LANES : (tile_at + 1) * LANES,
+        ] = sums[core, source]
+
+    for source in range(owners):
+        f_copy(source, 1 - s).wait_recv()
+    for source in range(owners):
+        for core in range(2):
+            place_piece(core, source)
+
+    def left(other):
+        @owns(other)
+        def _():
+            c_copy(other, chip).wait_send()
+
+        @owns(chip)
+        def _():
+            b_copy(other, chip).wait_send()
+
+    others(left)
+    for source in range(owners):
+        f_copy(source, s).wait_send()
 
     for d in range(2):
         @when(b + 1 - 2 * d)
@@ -277,12 +385,18 @@
         rows, wide = teacher_feats.shape
         sdim, edim = head_weight.shape
         depth = (wide + sdim) // LANES * (rows // CHUNKS) + STAT_ROWS
+        chips, tiles, half = n_batch * n_pair, edim // LANES, sdim // 2
+        piece = min(
+            size for size in range(STAT_ROWS, half + 1, STAT_ROWS)
+            if half % size == 0 and half // size * tiles <= chips
+        )
+        owners = half // piece * tiles
         vmem = pl.BlockSpec(memory_space=pltpu.VMEM)
-        student_grad, local_head = pl.pallas_call(
+        student_grad, head_sum = pl.pallas_call(
             functools.partial(kernel, n_batch, n_pair),
             out_shape=(
                 jax.ShapeDtypeStruct((rows, sdim), BF),
-                jax.ShapeDtypeStruct((sdim, edim), F32),
+                jax.ShapeDtypeStruct((sdim, edim), BF),
             ),
             in_specs=[vmem] * 5,
             out_specs=(vmem, vmem),
@@ -293,10 +407,23 @@
                 pltpu.VMEM((rows, edim), BF),
                 pltpu.VMEM((rows, edim), F32),
                 pltpu.VMEM((rows, edim), F32),
+                pltpu.VMEM((tiles, sdim, LANES), F32),
+                pltpu.VMEM((tiles, half, LANES), BF),
+                pltpu.VMEM((tiles, half, LANES), BF),
+                pltpu.VMEM((tiles, half, LANES), BF),
+                pltpu.VMEM((chips, piece, LANES), BF),
+                pltpu.VMEM((2, owners, piece, LANES), BF),
                 pltpu.SemaphoreType.DMA((2, hops, CHUNKS)),
                 pltpu.SemaphoreType.DMA((2, hops, n_pair, CHUNKS)),
                 pltpu.SemaphoreType.DMA((2, hops, n_pair, CHUNKS)),
                 pltpu.SemaphoreType.DMA((2, hops, n_pair, 2, CHUNKS)),
+                pltpu.SemaphoreType.DMA((1,)),
+                pltpu.SemaphoreType.DMA((1,)),
+                pltpu.SemaphoreType.DMA((chips,)),
+                pltpu.SemaphoreType.DMA((chips,)),
+                pltpu.SemaphoreType.DMA((chips,)),
+                pltpu.SemaphoreType.DMA((2, owners)),
+                pltpu.SemaphoreType.DMA((owners,)),
             ],
             compiler_params=pltpu.CompilerParams(
                 collective_id=0, has_side_effects=True, vmem_limit_bytes=56 * 1024 * 1024
@@ -305,7 +432,7 @@
             teacher_feats, student_feats, head_weight,
             teacher_lse.reshape(1, rows), student_lse.reshape(1, rows),
         )
-        head_grad = lax.psum(local_head, ("batch", "pair", "sub")) * HEAD_SCALE
+        head_grad = head_sum.astype(F32) * HEAD_SCALE
         return student_grad, head_grad
 
     in_specs = (

time: 160 us -> 74.5 us (0.47)
  the two profiles are of different devices: /device:TPU:0 before, /device:TPU:9 now
where the time goes in v2:
time: 74.5 us; the launch traced here: 74.3 us
  Pallas kernels  70.5 us (95%)
  other arithmetic  2.5 us (3%)
    pallas_call x1, Pallas kernels, body(): pl.pallas_call(functools.partial(kernel, n_batch, n_pair), out_shape=(jax...  70.5 us
    mul x1, other arithmetic, body(): head_grad = head_sum.astype(F32) * HEAD_SCALE  2.5 us

profile of v2, /device:TPU:9, one launch (start us, length us, event | category | flops | bytes accessed | tf_op | source)
XLA Modules:
  0.0 74.3 jit_solution(9772257350542935362)
XLA Ops:
  0.6 70.5 %shard_map.68 = (bf16[128,384]{1,0:T(8,128)(2,1)}, bf16[384,1024]{1,0:T(8,128)(2,1)}) custom-call(bf16[128,1024]{1,0:T(8,128)(2,1)} %tf_ref.1, bf16[128,384]{1,0:T(8,128)(2,1)} %sf_ref.1, bf16[384,1024]{1,0:T(8,128)(2,1)} %hw_ref.1, f32[1,128]{1,0:T(1,128)} %bitcast.2, f32[1,128]{1,0:T(1,128)} %bitcast.3), custom_call_target="tpu_custom_call" | custom-call | tf_op jit(solution)/shard_map/pallas_call | solution.py:395
  71.2 0.0 copy-start
  71.2 2.5 %convert_multiply_fusion = f32[384,1024]{1,0:T(8,128)} fusion(bf16[384,1024]{1,0:T(8,128)(2,1)} %get-tuple-element.5), kind=kLoop, calls=%fused_computation | loop fusion | flops 786432 | bytes 2359296 | tf_op jit(solution)/shard_map/mul | solution.py:435
  73.7 0.0 copy-done
  73.7 0.6 copy.8
Async XLA Ops:
  71.2 2.5 %copy-start = (bf16[128,384]{1,0:T(8,128)(2,1)S(1)}, bf16[128,384]{1,0:T(8,128)(2,1)}, u32[]{:S(2)}) copy-start(bf16[128,384]{1,0:T(8,128)(2,1)} %get-tuple-element.8) | copy-start | bytes 294916

commit v3 on v2

--- a/solution.py
+++ b/solution.py
@@ -243,15 +243,29 @@
             def _():
                 z_step(h, q)
 
-            if q == 0:
-                @pl.when(h > 0)
-                def _():
-                    x_step(h - 1, CHUNKS - 1)
-                    work(h - 1, 0, n_pair)
-            else:
+            if q > 0:
                 @pl.when(h < hops)
                 def _():
                     x_step(h, q - 1)
+
+            @pl.when(h > 0)
+            def _():
+                if q == 0:
+                    @pl.when(h == hops)
+                    def _():
+                        work(h - 1, 0, 1)
+
+                    x_step(h - 1, CHUNKS - 1)
+
+                    @pl.when(h == hops)
+                    def _():
+                        work(h - 1, 1, n_pair)
+
+                first, last = q * n_pair // CHUNKS, (q + 1) * n_pair // CHUNKS
+                if last > first:
+                    @pl.when(h < hops)
+                    def _():
+                        work(h - 1, first, last)
         return carry
 
     lax.fori_loop(0, hops + 1, stage, 0)

time: 74.5 us -> 72.9 us (0.979)
  Pallas kernels: 70.5 us -> 68.9 us
    pallas_call x1, Pallas kernels: 70.5 us -> 68.9 us  [body(): pl.pallas_call(functools.partial(kernel, n_batch, n_pair), out_shape=(jax...]
where the time goes in v3:
time: 72.9 us; the launch traced here: 72.7 us
  Pallas kernels  68.9 us (95%)
  other arithmetic  2.5 us (3%)
    pallas_call x1, Pallas kernels, body(): pl.pallas_call(functools.partial(kernel, n_batch, n_pair), out_shape=(jax...  68.9 us
    mul x1, other arithmetic, body(): head_grad = head_sum.astype(F32) * HEAD_SCALE  2.5 us

profile of v3, /device:TPU:9, one launch (start us, length us, event | category | flops | bytes accessed | tf_op | source)
XLA Modules:
  0.0 72.7 jit_solution(14879274658640143887)
XLA Ops:
  0.6 68.9 %shard_map.68 = (bf16[128,384]{1,0:T(8,128)(2,1)}, bf16[384,1024]{1,0:T(8,128)(2,1)}) custom-call(bf16[128,1024]{1,0:T(8,128)(2,1)} %tf_ref.1, bf16[128,384]{1,0:T(8,128)(2,1)} %sf_ref.1, bf16[384,1024]{1,0:T(8,128)(2,1)} %hw_ref.1, f32[1,128]{1,0:T(1,128)} %bitcast.2, f32[1,128]{1,0:T(1,128)} %bitcast.3), custom_call_target="tpu_custom_call" | custom-call | tf_op jit(solution)/shard_map/pallas_call | solution.py:409
  69.6 0.0 copy-start
  69.6 2.5 %convert_multiply_fusion = f32[384,1024]{1,0:T(8,128)} fusion(bf16[384,1024]{1,0:T(8,128)(2,1)} %get-tuple-element.5), kind=kLoop, calls=%fused_computation | loop fusion | flops 786432 | bytes 2359296 | tf_op jit(solution)/shard_map/mul | solution.py:449
  72.1 0.0 copy-done
  72.1 0.6 copy.8
Async XLA Ops:
  69.6 2.5 %copy-start = (bf16[128,384]{1,0:T(8,128)(2,1)S(1)}, bf16[128,384]{1,0:T(8,128)(2,1)}, u32[]{:S(2)}) copy-start(bf16[128,384]{1,0:T(8,128)(2,1)} %get-tuple-element.8) | copy-start | bytes 294916

commit v4 on v3

--- a/solution.py
+++ b/solution.py
@@ -16,6 +16,7 @@
 LANES = 128
 CHUNKS = 2
 STAT_ROWS = 16
+SWAPS = 2
 MESH = pl.DeviceIdType.MESH
 BF = jnp.bfloat16
 F32 = jnp.float32
@@ -280,16 +281,22 @@
 
     here = pl.ds(pl.multiple_of(s * half, STAT_ROWS), half)
     there = pl.ds(pl.multiple_of((1 - s) * half, STAT_ROWS), half)
-    half_out[...] = part[:, there, :].astype(BF)
-    swap = pltpu.make_async_remote_copy(
-        src_ref=half_out, dst_ref=half_in, send_sem=half_send.at[0], recv_sem=half_recv.at[0],
-        device_id={"sub": 1 - s}, device_id_type=MESH,
-    )
-    swap.start()
+    groups = half_send.shape[0]
+    share = tiles // groups
+
+    def swap(i):
+        at = pl.ds(i * share, share)
+        return pltpu.make_async_remote_copy(
+            src_ref=half_out.at[at], dst_ref=half_in.at[at],
+            send_sem=half_send.at[i], recv_sem=half_recv.at[i],
+            device_id={"sub": 1 - s}, device_id_type=MESH,
+        )
+
+    for i in range(groups):
+        at = slice(i * share, (i + 1) * share)
+        half_out[at] = part[at, there, :].astype(BF)
+        swap(i).start()
     sg_ref[...] = nt(grad_proj, hw_ref[...]).astype(BF)
-    swap.wait()
-    part[:, here, :] = part[:, here, :] + half_in[...].astype(F32)
-    mine[...] = part[:, here, :].astype(BF)
 
     def piece_of(index):
         return lax.rem(index, tiles), index // tiles * piece
@@ -322,7 +329,20 @@
         def _():
             c_copy(owner, chip).start()
 
-    others(scatter)
+    for i in range(groups):
+        at = slice(i * share, (i + 1) * share)
+        swap(i).wait()
+        part[at, here, :] = part[at, here, :] + half_in[at].astype(F32)
+        mine[at] = part[at, here, :].astype(BF)
+
+        def scatter_part(other):
+            tile_at = lax.rem(other, tiles)
+
+            @pl.when(jnp.logical_and(tile_at >= i * share, tile_at < (i + 1) * share))
+            def _():
+                scatter(other)
+
+        others(scatter_part)
 
     @owns(chip)
     def _():
@@ -330,7 +350,7 @@
         first = part[tile_at, pl.ds(pl.multiple_of(s * half + row_at, STAT_ROWS), piece), :]
 
         def add(k, total):
-            source = lax.rem(chip + k, chips)
+            source = lax.rem(chip + chips - k, chips)
             c_copy(chip, source).wait_recv()
             return total + chunks[source].astype(F32)
 
@@ -344,7 +364,11 @@
             b_copy(source, source).wait_recv()
             f_copy(source, s).start()
 
-    others(pass_on)
+    def in_order(k, carry):
+        pass_on(lax.rem(chip + chips - k, chips))
+        return carry
+
+    lax.fori_loop(1, chips, in_order, 0)
 
     def place_piece(core, source):
         tile_at, row_at = source % tiles, source // tiles * piece
@@ -431,8 +455,8 @@
                 pltpu.SemaphoreType.DMA((2, hops, n_pair, CHUNKS)),
                 pltpu.SemaphoreType.DMA((2, hops, n_pair, CHUNKS)),
                 pltpu.SemaphoreType.DMA((2, hops, n_pair, 2, CHUNKS)),
-                pltpu.SemaphoreType.DMA((1,)),
-                pltpu.SemaphoreType.DMA((1,)),
+                pltpu.SemaphoreType.DMA((SWAPS,)),
+                pltpu.SemaphoreType.DMA((SWAPS,)),
                 pltpu.SemaphoreType.DMA((chips,)),
                 pltpu.SemaphoreType.DMA((chips,)),
                 pltpu.SemaphoreType.DMA((chips,)),

time: 72.9 us -> 72.2 us (level)
  no operation moved by 1% of the time
where the time goes in v4:
time: 72.2 us; the launch traced here: 72 us
  Pallas kernels  68.2 us (94%)
  other arithmetic  2.5 us (3%)
    pallas_call x1, Pallas kernels, body(): pl.pallas_call(functools.partial(kernel, n_batch, n_pair), out_shape=(jax...  68.2 us
    mul x1, other arithmetic, body(): head_grad = head_sum.astype(F32) * HEAD_SCALE  2.5 us

profile of v4, /device:TPU:9, one launch (start us, length us, event | category | flops | bytes accessed | tf_op | source)
XLA Modules:
  0.0 72.0 jit_solution(1754130248649987765)
XLA Ops:
  0.6 68.2 %shard_map.68 = (bf16[128,384]{1,0:T(8,128)(2,1)}, bf16[384,1024]{1,0:T(8,128)(2,1)}) custom-call(bf16[128,1024]{1,0:T(8,128)(2,1)} %tf_ref.1, bf16[128,384]{1,0:T(8,128)(2,1)} %sf_ref.1, bf16[384,1024]{1,0:T(8,128)(2,1)} %hw_ref.1, f32[1,128]{1,0:T(1,128)} %bitcast.2, f32[1,128]{1,0:T(1,128)} %bitcast.3), custom_call_target="tpu_custom_call" | custom-call | tf_op jit(solution)/shard_map/pallas_call | solution.py:433
  68.9 0.0 copy-start
  68.9 2.5 %convert_multiply_fusion = f32[384,1024]{1,0:T(8,128)} fusion(bf16[384,1024]{1,0:T(8,128)(2,1)} %get-tuple-element.5), kind=kLoop, calls=%fused_computation | loop fusion | flops 786432 | bytes 2359296 | tf_op jit(solution)/shard_map/mul | solution.py:473
  71.4 0.0 copy-done
  71.4 0.6 copy.8
Async XLA Ops:
  68.9 2.5 %copy-start = (bf16[128,384]{1,0:T(8,128)(2,1)S(1)}, bf16[128,384]{1,0:T(8,128)(2,1)}, u32[]{:S(2)}) copy-start(bf16[128,384]{1,0:T(8,128)(2,1)} %get-tuple-element.8) | copy-start | bytes 294916
